TPU v7x, 256 devices: a whole 4x4x8 slice. The times are simulated.
256 devices in a mesh: brick: 32 (over z_hi, x, core), view: 8 (over y, z_lo).
Axes of the slice: x: 4, y: 4, z: 8 (z_hi: 4, z_lo: 2; z = z_hi * 2 + z_lo), core: 2. Of those that a mesh axis runs over, the one named last changes fastest.
Arguments:
- estimate: float32 [256, 64, 512], P('brick'), may hold values from 0.5 to 2
- camera_blocks: bfloat16 [8, 512, 8, 2048], P('view', 'brick'), may hold values from 0.099609375 to 2
- block_lists: int32 [8, 32, 32, 2], P('view'), may hold values from -1 to 15, as said below
- block_offsets: int32 [8, 512], P('view'), may hold values from 1 to 252, as said below
- psf_index: int32 [8, 64], P('view'), may hold values from 0 to 15
- psf_bank: float32 [8, 2, 16, 9], P('view'), may hold values from 0.03 to 0.3
Outputs:
- updated: float32 [256, 64, 512], P('brick')
Inputs may be any that keep to these rules, and one draw needn't show every extreme that they name: block_lists[v, d, s] names exactly the blocks of holder s that intersect brick d, each once; at most 2 of them, and 2 for some brick and holder. `block_offsets`: every block starts after its brick's first row by 1 to 4 rows.
All inputs are finite; a program needn't handle non-finite values.
Results may differ from a plain program's by a relative error of at most 0.0003.
Values may be sent and summed in bfloat16 or wider, within the bound.
A program may use at most 128 MiB of HBM per device.

v0:
```python
import jax
import jax.numpy as jnp
from jax import lax
from jax.sharding import PartitionSpec as P


def with_halo(cells, sides, width):
    for axis, dim in sides:
        count = lax.axis_size(axis)
        ends = count - 1
        head = lax.slice_in_dim(cells, 0, width, axis=dim)
        tail = lax.slice_in_dim(cells, cells.shape[dim] - width, cells.shape[dim], axis=dim)
        cells = jnp.concatenate(
            [
                lax.ppermute(tail, axis, [(i, (i + 1) % count) for i in range(ends)]),
                cells,
                lax.ppermute(head, axis, [((i + 1) % count, i) for i in range(ends)]),
            ],
            axis=dim,
        )
    return cells


def joined(value, axis, join):
    pieces = lax.all_gather(value, axis)
    head = pieces[0]
    tail = pieces[1:]
    running, _ = lax.scan(lambda running, slab: (join(running, slab), None), head, tail)
    return running


def blur_cols(field, kern, reverse):
    tap_count = kern.shape[1]
    radius = tap_count // 2
    width = field.shape[2]
    padded = jnp.pad(field, ((0, 0), (0, 0), (radius, radius)))
    result = None
    for offset in range(tap_count):
        begin_at = 2 * radius - offset if reverse else offset
        term = kern[:, offset][None, :, None] * padded[:, :, begin_at : begin_at + width]
        result = term if result is None else result + term
    return result


def blur_rows(padded, kern, reverse, rows):
    tap_count = kern.shape[1]
    radius = tap_count // 2
    result = None
    for offset in range(tap_count):
        begin_at = 2 * radius - offset if reverse else offset
        term = kern[:, offset][None, :, None] * padded[begin_at : begin_at + rows]
        result = term if result is None else result + term
    return result


def place_blocks(blocks, column_ids, row_starts, is_valid, start_x, rows_dev, depth, column_count):
    block_rows = blocks.shape[1]
    block_cols = column_count // 1
    local_rows = row_starts[:, None] + jnp.arange(block_rows, dtype=jnp.int32)[None, :] - start_x
    row_hit = (
        local_rows[:, :, None] == jnp.arange(rows_dev, dtype=jnp.int32)[None, None, :]
    ) & is_valid[:, None, None]
    colhot = column_ids[:, None] == jnp.arange(column_count, dtype=jnp.int32)[None, :]
    weight = (row_hit[:, :, :, None] & colhot[:, None, None, :]).astype(jnp.bfloat16)
    summed = jnp.einsum("sabc,saf->bcf", weight, blocks, preferred_element_type=jnp.float32)
    block_width = blocks.shape[2] // depth
    summed = summed.reshape(rows_dev, block_cols, depth, block_width)
    return summed.transpose(0, 2, 1, 3).reshape(rows_dev, depth, block_cols * block_width)


def multiply(first_value, second_value):
    return first_value * second_value


def shards(estimate, camera_blocks, block_lists, block_offsets, psf_index, psf_bank):
    rows_dev, depth, columns = estimate.shape
    tile_count = camera_blocks.shape[1]
    brick_here = lax.axis_index("brick")
    start_x = brick_here * rows_dev
    tap_count = psf_bank.shape[-1]
    radius = tap_count // 2
    kern_count = psf_bank.shape[2]
    kernel_pick = (
        psf_index[0][:, None] == jnp.arange(kern_count, dtype=jnp.int32)[None, :]
    ).astype(jnp.float32)
    kern_x = jnp.dot(kernel_pick, psf_bank[0, 0], precision=lax.Precision.HIGHEST)
    kern_y = jnp.dot(kernel_pick, psf_bank[0, 1], precision=lax.Precision.HIGHEST)
    offsets_view = block_offsets[0]
    gathered = lax.all_gather(camera_blocks, "brick", axis=1, tiled=True)
    count = gathered.shape[1]
    block_ids = jnp.arange(count, dtype=jnp.int32)
    measured = place_blocks(
        gathered[0],
        block_ids % tile_count,
        offsets_view,
        block_ids >= 0,
        start_x,
        rows_dev,
        depth,
        tile_count,
    )
    padded = with_halo(estimate, (("brick", 0),), radius)
    blurred = blur_rows(blur_cols(padded, kern_y, False), kern_x, False, rows_dev)
    ratio = measured / blurred
    padded_ratio = with_halo(ratio, (("brick", 0),), radius)
    correction = blur_rows(blur_cols(padded_ratio, kern_y, True), kern_x, True, rows_dev)
    product = joined(correction, "view", multiply)
    return estimate * product


def solution(mesh):
    placed = (
        P("brick", None, None),
        P("view", "brick", None, None),
        P("view", None, None, None),
        P("view", None),
        P("view", None),
        P("view", None, None, None),
    )
    return jax.shard_map(
        shards, mesh=mesh, in_specs=placed, out_specs=P("brick", None, None), check_vma=False
    )
```

profile of v0, /device:TPU:1, one launch (start us, length us, event | category | flops | bytes accessed | tf_op | source)
XLA Modules:
  0.0 433.1 jit_solution(10102572551987792969)
XLA Ops:
  6.5 0.7 all-gather.4.cloned.1.call-update
  7.3 0.0 all-gather.6.cloned.1.call-start
  7.3 2.1 fusion.49
  9.4 4.5 %collective-permute-start = (f32[4,64,512]{2,1,0:T(8,128)S(1)}, f32[4,64,512]{2,1,0:T(8,128)}, u32[]{:S(2)}, u32[]{:S(2)}) collective-permute-start(f32[4,64,512]{2,1,0:T(8,128)S(1)} %get-tuple-element.34), channel_id=1, source_target_pairs={{0,8},{8,16},{16,24},{24,32},{32,40},{40,48},{48,56},{56,64},{64,7... | collective-permute-start | bytes 1572872 | tf_op jit(solution)/shard_map/ppermute | solution.py:15
  13.9 2.7 collective-permute-start.1
  16.6 0.8 fusion.50
  17.4 0.1 copy.32
  17.5 0.1 copy.33
  17.6 0.8 fusion.40
  18.5 0.9 fusion.39
  19.4 1.8 copy.23
  21.3 0.0 collective-permute-done
  21.3 1.4 copy.22
  22.7 2.1 collective-permute-done.1
  24.7 2.4 copy.24
  27.1 1.7 pad_maximum_fusion
  28.8 6.2 %multiply_add_fusion.1 = f32[16,64,512]{1,2,0:T(8,128)} fusion(f32[16,64,512]{1,2,0:T(8,128)S(1)} %pad_maximum_fusion, f32[64]{0:T(128)S(1)} %get-tuple-element.48, f32[64]{0:T(128)S(1)} %get-tuple-element.49, f32[64]{0:T(128)S(1)} %get-tuple-element.50, f32[64]{0:T(128)S(1)} %get-tuple-element.51, f32[64]{0:T(128)S(1)} %get-tuple-element.52, ...), kind=kLoop, calls=%fused_computation.15 | loop fusion | flops 8912896 | bytes 4196608 | tf_op jit(solution)/shard_map/add | solution.py:41
  35.0 95.8 %all-gather.4.cloned.1.call-done = bf16[1,512,8,2048]{3,2,0,1:T(8,128)(2,1)} async-done(((bf16[1,16,8,2048]{3,2,0,1:T(8,128)(2,1)}), bf16[1,512,8,2048]{3,2,0,1:T(8,128)(2,1)}) %all-gather.4.cloned.1.call-update) | async-done | bytes 16777232 | tf_op jit(solution)/shard_map/all_gather | solution.py:89
  130.8 25.6 %copy.19 = bf16[1,512,8,2048]{1,2,3,0:T(8,128)(2,1)} copy(bf16[1,512,8,2048]{3,2,0,1:T(8,128)(2,1)} %all-gather.4.cloned.1.call-done) | data formatting | bytes 33554432 | tf_op jit(solution)/shard_map/all_gather | solution.py:89
  156.4 29.9 %fusion.32 = f32[8,64,16,32]{1,2,3,0:T(8,128)S(1)} fusion(bf16[64,32,8,512]{3,2,1,0:T(8,128)(2,1)} %bitcast.75, pred[512,16]{0,1:T(8,128)(4,1)S(1)} %iota_compare_fusion.1, pred[512,8,8]{0,1,2:T(8,128)(4,1)S(1)} %iota_compare_fusion), kind=kOutput, calls=%fused_computation.61 | convolution fusion | flops 2148007936 | bytes 17866752 | tf_op jit(solution)/shard_map/sabc,saf->bcf/dot_general | solution.py:65
  186.3 0.6 copy.21
  186.9 1.5 copy-done
  188.4 1.7 fusion.22
  190.2 1.1 fusion.48
  191.3 2.3 copy.26
  193.6 2.3 collective-permute-start.3
  196.0 1.1 copy.25
  197.1 3.4 collective-permute-start.2
  200.5 4.0 collective-permute-done.3
  204.4 1.4 copy.28
  205.8 1.1 collective-permute-done.2
  206.9 2.4 copy.27
  209.2 1.7 pad_maximum_fusion.1
  210.9 5.3 %multiply_add_fusion = f32[16,64,512]{1,2,0:T(8,128)S(1)} fusion(f32[16,64,512]{1,2,0:T(8,128)S(1)} %pad_maximum_fusion.1, f32[64]{0:T(128)S(1)} %get-tuple-element.48, f32[64]{0:T(128)S(1)} %get-tuple-element.49, f32[64]{0:T(128)S(1)} %get-tuple-element.50, f32[64]{0:T(128)S(1)} %get-tuple-element.51, f32[64]{0:T(128)S(1)} %get-tuple-element.52, ...), kind=kLoop, calls=%fused_computation.6 | loop fusion | flops 8912896 | bytes 4196608 | tf_op jit(solution)/shard_map/add | solution.py:41
  216.2 1.3 fusion.13
  217.5 1.6 copy.29
  219.1 0.0 all-gather.6.cloned.1.call-update
  219.1 187.4 %all-gather.6.cloned.1.call-done = f32[64,64,512]{2,1,0:T(8,128)} async-done(((f32[8,64,512]{2,1,0:T(8,128)}), f32[64,64,512]{2,1,0:T(8,128)}) %all-gather.6.cloned.1.call-update) | async-done | bytes 8388624 | tf_op jit(solution)/shard_map/all_gather | solution.py:25
  406.6 7.7 %slice.301 = f32[56,64,512]{2,1,0:T(8,128)} slice(f32[64,64,512]{2,1,0:T(8,128)} %all-gather.6.cloned.1.call-done), slice={[8:64], [0:64], [0:512]} | slice | bytes 14680064 | tf_op jit(solution)/shard_map/slice | solution.py:27
  414.2 10.7 %while.10 = (s32[]{:T(128)}, f32[8,64,512]{2,1,0:T(8,128)S(1)}, f32[7,8,64,512]{3,2,1,0:T(8,128)}, s32[]{:T(128)}) while((s32[]{:T(128)}, f32[8,64,512]{2,1,0:T(8,128)S(1)}, f32[7,8,64,512]{3,2,1,0:T(8,128)}, s32[]{:T(128)}) %tuple.46), condition=%wide.region_1.2_spmd, body=%wide.region_0.1_spmd.sunk | while | flops 262146 | bytes 3145793 | solution.py:28
  414.3 1.6 bitcast_multiply_fusion.2
  415.9 1.5 bitcast_multiply_fusion.2
  417.4 1.5 bitcast_multiply_fusion.2
  418.9 1.5 bitcast_multiply_fusion.2
  420.4 1.5 bitcast_multiply_fusion.2
  421.9 1.5 bitcast_multiply_fusion.2
  423.5 1.5 bitcast_multiply_fusion.2
  425.0 1.2 mul.370
  (14 shorter events, 0.1 us)
Async XLA Ops:
  6.5 14.7 %copy-start.2 = (s32[1,512]{1,0:T(1,128)S(1)}, s32[1,512]{1,0:T(1,128)}, u32[]{:S(2)}) copy-start(s32[1,512]{1,0:T(1,128)} %param.10) | copy-start | bytes 6148
  6.5 124.3 %all-gather.4.cloned.1.call-start = ((), (), s32[]{:S(2)}) async-start(), calls=%async_computation | async-start | bytes 17301504 | tf_op jit(solution)/shard_map/all_gather | solution.py:89
  7.3 399.3 %all-gather.6.cloned.1.call-start = ((), (), s32[]{:S(2)}) async-start(), calls=%async_computation.1 | async-start | bytes 9437184 | tf_op jit(solution)/shard_map/all_gather | solution.py:25
  9.4 11.9 %collective-permute-start = (f32[4,64,512]{2,1,0:T(8,128)S(1)}, f32[4,64,512]{2,1,0:T(8,128)}, u32[]{:S(2)}, u32[]{:S(2)}) collective-permute-start(f32[4,64,512]{2,1,0:T(8,128)S(1)} %get-tuple-element.34), channel_id=1, source_target_pairs={{0,8},{8,16},{16,24},{24,32},{32,40},{40,48},{48,56},{56,64},{64,7... | collective-permute-start | bytes 1572872 | tf_op jit(solution)/shard_map/ppermute | solution.py:15
  13.9 10.8 %collective-permute-start.1 = (f32[4,64,512]{2,1,0:T(8,128)}, f32[4,64,512]{2,1,0:T(8,128)}, u32[]{:S(2)}, u32[]{:S(2)}) collective-permute-start(f32[4,64,512]{2,1,0:T(8,128)} %get-tuple-element.35), channel_id=1, source_target_pairs={{8,0},{16,8},{24,16},{32,24},{40,32},{48,40},{56,48},{64,56},{72,6... | collective-permute-start | bytes 1572872 | tf_op jit(solution)/shard_map/ppermute | solution.py:17
  186.2 2.2 copy-start
  193.6 10.8 %collective-permute-start.3 = (f32[4,64,512]{2,1,0:T(8,128)}, f32[4,64,512]{2,1,0:T(8,128)}, u32[]{:S(2)}, u32[]{:S(2)}) collective-permute-start(f32[4,64,512]{2,1,0:T(8,128)} %copy.26), channel_id=1, source_target_pairs={{8,0},{16,8},{24,16},{32,24},{40,32},{48,40},{56,48},{64,56},{72,6... | collective-permute-start | bytes 1572872 | tf_op jit(solution)/shard_map/ppermute | solution.py:17
  197.1 9.8 %collective-permute-start.2 = (f32[4,64,512]{2,1,0:T(8,128)}, f32[4,64,512]{2,1,0:T(8,128)}, u32[]{:S(2)}, u32[]{:S(2)}) collective-permute-start(f32[4,64,512]{2,1,0:T(8,128)} %copy.25), channel_id=1, source_target_pairs={{0,8},{8,16},{16,24},{24,32},{32,40},{40,48},{48,56},{56,64},{64,7... | collective-permute-start | bytes 1572872 | tf_op jit(solution)/shard_map/ppermute | solution.py:15
  406.6 7.7 %slice-start = ((f32[64,64,512]{2,1,0:T(8,128)}), f32[8,64,512]{2,1,0:T(8,128)S(1)}, s32[]{:S(2)}) async-start(f32[64,64,512]{2,1,0:T(8,128)} %all-gather.6.cloned.1.call-done), calls=%async_computation.2 | async-start | bytes 2097152 | tf_op jit(solution)/shard_map/slice | solution.py:26
  414.2 10.7 %copy-start.1 = (f32[8,64,512]{2,1,0:T(8,128)S(1)}, f32[8,64,512]{2,1,0:T(8,128)}, u32[]{:S(2)}) copy-start(f32[8,64,512]{2,1,0:T(8,128)} %param.8) | copy-start | bytes 3145732
Sparse Core Ops, SparseCore 0:
  9.9 120.8 all-gather.3
  219.2 187.2 all-gather.5
where the time goes:
time: 435 us; the launch traced here: 433 us
  waiting for transfers between devices  291 us (67%)
  local copies, waits for them, and re-layouts  54 us (12%)
  matrix products  31.6 us (7%)
  other arithmetic  29.8 us (7%)
  between operations  13.6 us (3%)
  starting transfers between devices  13 us (3%)
    all_gather x1, waiting for transfers between devices, joined(): pieces = lax.all_gather(value, axis)  187 us
    all_gather x1, waiting for transfers between devices, shards(): gathered = lax.all_gather(camera_blocks, 'brick', axis=1, tiled=True)  95.8 us
    dot_general x1, matrix products, place_blocks(): jnp.einsum('sabc,saf->bcf', weight, blocks, preferred_element_type=jnp.fl...  29.9 us
    all_gather x1, local copies, waits for them, and re-layouts, shards(): gathered = lax.all_gather(camera_blocks, 'brick', axis=1, tiled=True)  25.6 us
    add x2, other arithmetic, blur_cols(): result = term if result is None else result + term  11.4 us
    mul x7, other arithmetic, multiply(): return first_value * second_value  10.6 us
  transfers between devices with their start and end apart: 6, of which 5 were waited for; matrix products, arithmetic and copies ran while one was open for 5% of the time, Pallas kernels for 0%

commit v1 on v0

--- a/solution.py
+++ b/solution.py
@@ -86,7 +86,9 @@
     kern_x = jnp.dot(kernel_pick, psf_bank[0, 0], precision=lax.Precision.HIGHEST)
     kern_y = jnp.dot(kernel_pick, psf_bank[0, 1], precision=lax.Precision.HIGHEST)
     offsets_view = block_offsets[0]
-    gathered = lax.all_gather(camera_blocks, "brick", axis=1, tiled=True)
+    gathered = jnp.concatenate(
+        lax.all_to_all(jnp.stack([camera_blocks] * lax.axis_size("brick")), "brick", 0, 0), axis=1
+    )
     count = gathered.shape[1]
     block_ids = jnp.arange(count, dtype=jnp.int32)
     measured = place_blocks(

time: 435 us -> 715 us (1.64)
  waiting for transfers between devices: 291 us -> 554 us
  starting transfers between devices: 13 us -> 24.1 us
  local copies, waits for them, and re-layouts: 54 us -> 61.3 us
    all_to_all x0 -> x1, waiting for transfers between devices: none -> 253 us  [shards(): lax.all_to_all(jnp.stack([camera_blocks] * lax.axis_size('brick')), 'bric...]
    all_gather x1 -> x0, waiting for transfers between devices: 95.8 us -> none  [shards(): gathered = lax.all_gather(camera_blocks, 'brick', axis=1, tiled=True)]
    ppermute x2, waiting for transfers between devices: 1.09 us -> 78.8 us  [with_halo(): lax.ppermute(tail, axis, [(i, (i + 1) % count) for i in range(ends)])]
    all_gather x1 -> x0, local copies, waits for them, and re-layouts: 25.6 us -> none  [shards(): gathered = lax.all_gather(camera_blocks, 'brick', axis=1, tiled=True)]
    dot_general x0 -> x1, local copies, waits for them, and re-layouts: none -> 25.6 us  [place_blocks(): jnp.einsum('sabc,saf->bcf', weight, blocks, preferred_element_type=jnp.fl...]
    all_gather x1, waiting for transfers between devices: 187 us -> 203 us  [joined(): pieces = lax.all_gather(value, axis)]
    ppermute x2, waiting for transfers between devices: 6.01 us -> 19.9 us  [with_halo(): lax.ppermute(head, axis, [((i + 1) % count, i) for i in range(ends)])]
    all_to_all x0 -> x1, starting transfers between devices: none -> 12.8 us  [shards(): lax.all_to_all(jnp.stack([camera_blocks] * lax.axis_size('brick')), 'bric...]
  transfers between devices with their start and end apart: 6 -> 6, of which waited for: 5 -> 6; matrix products, arithmetic and copies ran while one was open for 5% -> 3% of each run, Pallas kernels for 0% -> 0%
where the time goes in v1:
time: 715 us; the launch traced here: 714 us
  waiting for transfers between devices  554 us (77%)
  local copies, waits for them, and re-layouts  61.3 us (9%)
  other arithmetic  30.3 us (4%)
  matrix products  30.3 us (4%)
  starting transfers between devices  24.1 us (3%)
  between operations  13.6 us (2%)
    all_to_all x1, waiting for transfers between devices, shards(): lax.all_to_all(jnp.stack([camera_blocks] * lax.axis_size('brick')), 'bric...  253 us
    all_gather x1, waiting for transfers between devices, joined(): pieces = lax.all_gather(value, axis)  203 us
    ppermute x2, waiting for transfers between devices, with_halo(): lax.ppermute(tail, axis, [(i, (i + 1) % count) for i in range(ends)])  78.8 us
    dot_general x1, matrix products, place_blocks(): jnp.einsum('sabc,saf->bcf', weight, blocks, preferred_element_type=jnp.fl...  29.9 us
    dot_general x1, local copies, waits for them, and re-layouts, place_blocks(): jnp.einsum('sabc,saf->bcf', weight, blocks, preferred_element_type=jnp.fl...  25.6 us
    ppermute x2, waiting for transfers between devices, with_halo(): lax.ppermute(head, axis, [((i + 1) % count, i) for i in range(ends)])  19.9 us
  transfers between devices with their start and end apart: 6, of which 6 were waited for; matrix products, arithmetic and copies ran while one was open for 3% of the time, Pallas kernels for 0%

profile of v1, /device:TPU:1, one launch (start us, length us, event | category | flops | bytes accessed | tf_op | source)
XLA Modules:
  0.0 713.6 jit_solution(9467658894080975121)
XLA Ops:
  6.5 6.8 stack.2
  13.3 12.8 %all-to-all-start = ((bf16[32,1,16,8,2048]{4,3,2,1,0:T(8,128)(2,1)}), bf16[32,1,16,8,2048]{4,3,2,1,0:T(8,128)(2,1)}, u32[]{:S(2)}, u32[]{:S(2)}) async-start(bf16[32,1,16,8,2048]{4,3,2,1,0:T(8,128)(2,1)} %stack.2), calls=%async_computation | async-start | bytes 33554432 | tf_op jit(solution)/shard_map/all_to_all | solution.py:90
  26.1 0.0 all-gather.3.cloned.1.call-start
  26.2 1.1 fusion.49
  27.3 3.5 collective-permute-start
  30.8 1.9 collective-permute-start.1
  32.7 0.1 copy.42
  32.8 0.1 copy.41
  32.9 0.2 fusion.39
  33.2 0.2 fusion.40
  33.4 0.6 copy.32
  34.1 76.8 %collective-permute-done = f32[4,64,512]{2,1,0:T(8,128)} collective-permute-done((f32[4,64,512]{2,1,0:T(8,128)}, f32[4,64,512]{2,1,0:T(8,128)}, u32[]{:S(2)}, u32[]{:S(2)}) %collective-permute-start) | collective-permute-done | bytes 524320 | tf_op jit(solution)/shard_map/ppermute | solution.py:15
  110.9 2.4 copy.31
  113.3 15.3 %collective-permute-done.1 = f32[4,64,512]{2,1,0:T(8,128)} collective-permute-done((f32[4,64,512]{2,1,0:T(8,128)}, f32[4,64,512]{2,1,0:T(8,128)}, u32[]{:S(2)}, u32[]{:S(2)}) %collective-permute-start.1) | collective-permute-done | bytes 524320 | tf_op jit(solution)/shard_map/ppermute | solution.py:17
  128.6 2.4 copy.33
  130.9 1.9 pad_maximum_fusion
  132.8 6.3 multiply_add_fusion.1
  139.2 252.6 %all-to-all-done = bf16[32,1,16,8,2048]{4,3,2,1,0:T(8,128)(2,1)} async-done(((bf16[32,1,16,8,2048]{4,3,2,1,0:T(8,128)(2,1)}), bf16[32,1,16,8,2048]{4,3,2,1,0:T(8,128)(2,1)}, u32[]{:S(2)}, u32[]{:S(2)}) %all-to-all-start) | async-done | bytes 16777248 | tf_op jit(solution)/shard_map/all_to_all | solution.py:90
  391.8 25.6 %copy.28 = bf16[2048,8,512]{2,1,0:T(8,128)(2,1)} copy(bf16[2048,8,512]{0,1,2:T(8,128)(2,1)} %bitcast.11) | data formatting | bytes 33554432 | tf_op jit(solution)/shard_map/sabc,saf->bcf/dot_general | solution.py:65
  417.3 29.9 %fusion.32 = f32[8,64,16,32]{1,2,3,0:T(8,128)S(1)} fusion(bf16[64,32,8,512]{3,2,1,0:T(8,128)(2,1)} %bitcast.74, pred[512,16]{0,1:T(8,128)(4,1)S(1)} %iota_compare_fusion.1, pred[512,8,8]{0,1,2:T(8,128)(4,1)S(1)} %iota_compare_fusion), kind=kOutput, calls=%fused_computation.61 | convolution fusion | flops 2148007936 | bytes 17866752 | tf_op jit(solution)/shard_map/sabc,saf->bcf/dot_general | solution.py:65
  447.2 0.6 copy.30
  447.9 1.5 copy-done
  449.4 1.7 fusion.22
  451.1 1.5 fusion.48
  452.6 2.3 copy.34
  455.0 3.9 collective-permute-start.2
  458.9 2.3 copy.35
  461.2 1.9 collective-permute-start.3
  463.1 1.9 collective-permute-done.2
  465.1 2.4 copy.36
  467.4 4.6 collective-permute-done.3
  472.0 2.4 copy.37
  474.4 1.9 pad_maximum_fusion.1
  476.3 5.3 multiply_add_fusion
  481.5 1.3 fusion.13
  482.9 1.6 copy.38
  484.5 0.0 all-gather.3.cloned.1.call-update
  484.5 202.7 %all-gather.3.cloned.1.call-done = f32[64,64,512]{2,1,0:T(8,128)} async-done(((f32[8,64,512]{2,1,0:T(8,128)}), f32[64,64,512]{2,1,0:T(8,128)}) %all-gather.3.cloned.1.call-update) | async-done | bytes 8388624 | tf_op jit(solution)/shard_map/all_gather | solution.py:25
  687.2 7.7 %slice.301 = f32[56,64,512]{2,1,0:T(8,128)} slice(f32[64,64,512]{2,1,0:T(8,128)} %all-gather.3.cloned.1.call-done), slice={[8:64], [0:64], [0:512]} | slice | bytes 14680064 | tf_op jit(solution)/shard_map/slice | solution.py:27
  694.9 10.6 %while.10 = (s32[]{:T(128)}, f32[8,64,512]{2,1,0:T(8,128)S(1)}, f32[7,8,64,512]{3,2,1,0:T(8,128)}, s32[]{:T(128)}) while((s32[]{:T(128)}, f32[8,64,512]{2,1,0:T(8,128)S(1)}, f32[7,8,64,512]{3,2,1,0:T(8,128)}, s32[]{:T(128)}) %tuple.45), condition=%wide.region_1.2_spmd, body=%wide.region_0.1_spmd.sunk | while | flops 262146 | bytes 3145785 | solution.py:28
  694.9 1.5 bitcast_multiply_fusion.2
  696.4 1.5 bitcast_multiply_fusion.2
  697.9 1.5 bitcast_multiply_fusion.2
  699.5 1.5 bitcast_multiply_fusion.2
  701.0 1.5 bitcast_multiply_fusion.2
  702.5 1.5 bitcast_multiply_fusion.2
  704.0 1.5 bitcast_multiply_fusion.2
  705.5 1.2 mul.370
  (18 shorter events, 0.1 us)
Async XLA Ops:
  13.3 12.9 %copy-start.1 = (f32[8,64,512]{2,1,0:T(8,128)S(1)}, f32[8,64,512]{2,1,0:T(8,128)}, u32[]{:S(2)}) copy-start(f32[8,64,512]{2,1,0:T(8,128)} %param.8) | copy-start | bytes 3145732
  13.3 19.4 %copy-start.2 = (f32[1,2,16,9]{2,1,3,0:T(2,128)S(1)}, f32[1,2,16,9]{2,1,3,0:T(2,128)}, u32[]{:S(2)}) copy-start(f32[1,2,16,9]{2,1,3,0:T(2,128)} %param.12) | copy-start | bytes 3460
  13.3 19.6 %copy-start.4 = (s32[1,64]{1,0:T(1,128)S(1)}, s32[1,64]{1,0:T(1,128)}, u32[]{:S(2)}) copy-start(s32[1,64]{1,0:T(1,128)} %param.11) | copy-start | bytes 772
  13.3 378.5 %all-to-all-start = ((bf16[32,1,16,8,2048]{4,3,2,1,0:T(8,128)(2,1)}), bf16[32,1,16,8,2048]{4,3,2,1,0:T(8,128)(2,1)}, u32[]{:S(2)}, u32[]{:S(2)}) async-start(bf16[32,1,16,8,2048]{4,3,2,1,0:T(8,128)(2,1)} %stack.2), calls=%async_computation | async-start | bytes 33554432 | tf_op jit(solution)/shard_map/all_to_all | solution.py:90
  26.1 7.9 %copy-start.3 = (s32[1,512]{1,0:T(1,128)S(1)}, s32[1,512]{1,0:T(1,128)}, u32[]{:S(2)}) copy-start(s32[1,512]{1,0:T(1,128)} %param.10) | copy-start | bytes 6148
  26.1 661.1 %all-gather.3.cloned.1.call-start = ((), (), s32[]{:S(2)}) async-start(), calls=%async_computation.1 | async-start | bytes 9437184 | tf_op jit(solution)/shard_map/all_gather | solution.py:25
  27.3 83.6 %collective-permute-start = (f32[4,64,512]{2,1,0:T(8,128)}, f32[4,64,512]{2,1,0:T(8,128)}, u32[]{:S(2)}, u32[]{:S(2)}) collective-permute-start(f32[4,64,512]{2,1,0:T(8,128)} %get-tuple-element.37), channel_id=1, source_target_pairs={{0,8},{8,16},{16,24},{24,32},{32,40},{40,48},{48,56},{56,64},{64,7... | collective-permute-start | bytes 1572872 | tf_op jit(solution)/shard_map/ppermute | solution.py:15
  30.8 97.8 %collective-permute-start.1 = (f32[4,64,512]{2,1,0:T(8,128)}, f32[4,64,512]{2,1,0:T(8,128)}, u32[]{:S(2)}, u32[]{:S(2)}) collective-permute-start(f32[4,64,512]{2,1,0:T(8,128)} %get-tuple-element.38), channel_id=1, source_target_pairs={{8,0},{16,8},{24,16},{32,24},{40,32},{48,40},{56,48},{64,56},{72,6... | collective-permute-start | bytes 1572872 | tf_op jit(solution)/shard_map/ppermute | solution.py:17
  447.2 2.2 copy-start
  455.0 10.1 %collective-permute-start.2 = (f32[4,64,512]{2,1,0:T(8,128)}, f32[4,64,512]{2,1,0:T(8,128)}, u32[]{:S(2)}, u32[]{:S(2)}) collective-permute-start(f32[4,64,512]{2,1,0:T(8,128)} %copy.34), channel_id=1, source_target_pairs={{0,8},{8,16},{16,24},{24,32},{32,40},{40,48},{48,56},{56,64},{64,7... | collective-permute-start | bytes 1572872 | tf_op jit(solution)/shard_map/ppermute | solution.py:15
  461.2 10.8 %collective-permute-start.3 = (f32[4,64,512]{2,1,0:T(8,128)}, f32[4,64,512]{2,1,0:T(8,128)}, u32[]{:S(2)}, u32[]{:S(2)}) collective-permute-start(f32[4,64,512]{2,1,0:T(8,128)} %copy.35), channel_id=1, source_target_pairs={{8,0},{16,8},{24,16},{32,24},{40,32},{48,40},{56,48},{64,56},{72,6... | collective-permute-start | bytes 1572872 | tf_op jit(solution)/shard_map/ppermute | solution.py:17
  687.2 7.7 %slice-start = ((f32[64,64,512]{2,1,0:T(8,128)}), f32[8,64,512]{2,1,0:T(8,128)S(1)}, s32[]{:S(2)}) async-start(f32[64,64,512]{2,1,0:T(8,128)} %all-gather.3.cloned.1.call-done), calls=%async_computation.2 | async-start | bytes 2097152 | tf_op jit(solution)/shard_map/slice | solution.py:26
Sparse Core Ops, SparseCore 0:
  484.6 202.5 all-gather.2
